TPU v7x, 256 devices: a whole 4x4x8 slice. The times are simulated.
256 devices in a mesh: blk: 128 (over x, y_lo, z, core), rep: 2 (over y_hi).
Axes of the slice: x: 4, y: 4 (y_hi: 2, y_lo: 2; y = y_hi * 2 + y_lo), z: 8, core: 2. Of those that a mesh axis runs over, the one named last changes fastest.
Arguments:
- photo_vectors: bfloat16 [131072, 1152], P(('blk', 'rep')), may hold values from -3.6 to 3.6
- caption_vectors: bfloat16 [131072, 1152], P(('blk', 'rep')), may hold values from -3.6 to 3.6
- exponent_of_scale: float32 [1], replicated, may hold values from 1.609 to 2.708
- additive_intercept: float32 [1], replicated, may hold values from -3 to -1
Outputs:
- grad_images: bfloat16 [131072, 1152], P(('blk', 'rep'))
- grad_captions: bfloat16 [131072, 1152], P(('blk', 'rep'))
All inputs are finite; a program needn't handle non-finite values.
Results may differ from a plain program's by a relative error of at most 0.009.
Values may be sent and summed in bfloat16 or wider, within the bound.
A program may use at most 128 MiB of HBM per device.

v0:
```python
import jax
import jax.numpy as jnp
from jax import lax
from jax.sharding import PartitionSpec as P


def padded(block, sides, width):
    for axis, dim in sides:
        count = lax.axis_size(axis)
        forward = [(i, i + 1) for i in range(count - 1)]
        forward.append((count - 1, 0))
        backward = [(target, source) for source, target in forward]
        low = lax.ppermute(
            lax.slice_in_dim(block, block.shape[dim] - width, None, axis=dim), axis, forward
        )
        high = lax.ppermute(lax.slice_in_dim(block, 0, width, axis=dim), axis, backward)
        block = jnp.concatenate([low, block, high], axis=dim)
    return block


def shifted(value, axis, steps):
    count = lax.axis_size(axis)
    pairs = [(source, (source + steps) % count) for source in range(count)]
    return lax.ppermute(value, axis, pairs)


def unit_rows(values):
    inverse = lax.rsqrt(jnp.sum(values * values, axis=1, keepdims=True) + 1e-06)
    return (values * inverse, inverse)


def back_rows(upstream, direction, inverse):
    return inverse * (upstream - direction * jnp.sum(upstream * direction, axis=1, keepdims=True))


def entry_coefficient(similarity_matrix, agreeing_couples, similarity_scale):
    target_polarity = jnp.where(agreeing_couples, 1.0, -1.0).astype(jnp.float32)
    return (
        similarity_scale * -target_polarity * jax.nn.sigmoid(-target_polarity * similarity_matrix)
    ).astype(jnp.bfloat16)


def shards(photo_vectors, caption_vectors, exponent_of_scale, additive_intercept):
    row_count = photo_vectors.shape[0]
    image_dir, image_inverse = unit_rows(photo_vectors.astype(jnp.float32))
    caption_dir, caption_inverse = unit_rows(caption_vectors.astype(jnp.float32))
    image_unit = image_dir.astype(jnp.bfloat16)
    caption_unit = caption_dir.astype(jnp.bfloat16)
    similarity_scale = jnp.exp(exponent_of_scale[0])
    moved_intercept = additive_intercept[0]
    caption_slice_entries = lax.all_gather(caption_unit, "rep", axis=0, tiled=True)
    block_rows = caption_slice_entries.shape[0]
    row_offset = lax.axis_index("rep") * row_count
    window = padded(caption_slice_entries, (("blk", 0),), block_rows)
    similarity_matrix = (
        similarity_scale
        * jnp.einsum("dn,ln->dl", image_unit, window, preferred_element_type=jnp.float32)
        + moved_intercept
    )
    row_index = lax.broadcasted_iota(jnp.int32, similarity_matrix.shape, 0)
    col_index = lax.broadcasted_iota(jnp.int32, similarity_matrix.shape, 1)
    agreeing_couples = col_index == row_index + block_rows + row_offset
    logistic_factor = entry_coefficient(similarity_matrix, agreeing_couples, similarity_scale)
    unit_grad_images = jnp.einsum(
        "ij,jd->id", logistic_factor, window, preferred_element_type=jnp.float32
    )
    partial_grads = jnp.einsum(
        "ij,id->jd", logistic_factor, image_unit, preferred_element_type=jnp.float32
    )
    from_upper = shifted(partial_grads[:block_rows].astype(jnp.bfloat16), "blk", -1).astype(
        jnp.float32
    )
    from_lower = shifted(partial_grads[2 * block_rows :].astype(jnp.bfloat16), "blk", 1).astype(
        jnp.float32
    )
    caption_terms = partial_grads[block_rows : 2 * block_rows] + from_upper + from_lower
    unit_grad_captions = lax.psum_scatter(caption_terms, "rep", scatter_dimension=0, tiled=True)
    grad_images = back_rows(unit_grad_images, image_dir, image_inverse).astype(jnp.bfloat16)
    grad_captions = back_rows(unit_grad_captions, caption_dir, caption_inverse).astype(jnp.bfloat16)
    return (grad_images, grad_captions)


def solution(mesh):
    return jax.shard_map(
        shards,
        mesh=mesh,
        in_specs=(P(("blk", "rep"), None), P(("blk", "rep"), None), P(), P()),
        out_specs=(P(("blk", "rep"), None), P(("blk", "rep"), None)),
        check_vma=False,
    )
```

profile of v0, /device:TPU:1, one launch (start us, length us, event | category | flops | bytes accessed | tf_op | source)
XLA Modules:
  0.0 215.6 jit_solution(8588883123431746536)
XLA Ops:
  7.2 0.0 copy-start.1
  7.2 0.0 all-gather.2.cloned.1.call-start
  7.2 1.7 fusion.16
  8.9 2.6 %fusion.3 = bf16[512,1152]{1,0:T(8,128)(2,1)} fusion(bf16[512,1152]{1,0:T(8,128)(2,1)} %param.5, f32[512]{0:T(512)S(1)} %add_rsqrt_fusion), kind=kLoop, calls=%fused_computation.8 | loop fusion | flops 1769472 | bytes 2361344 | tf_op jit(solution)/shard_map/convert_element_type | solution.py:48
  11.4 0.0 all-gather.2.cloned.1.call-update
  11.5 0.0 reduce-scatter.2.cloned.1.call-start
  11.5 46.6 %all-gather.2.cloned.1.call-done = bf16[1024,1152]{1,0:T(8,128)(2,1)} async-done(((bf16[512,1152]{1,0:T(8,128)(2,1)}), bf16[1024,1152]{1,0:T(8,128)(2,1)}) %all-gather.2.cloned.1.call-update) | async-done | bytes 2359312 | tf_op jit(solution)/shard_map/all_gather | solution.py:51
  58.1 1.8 collective-permute-start
  59.9 0.0 collective-permute-start.1
  61.3 0.0 copy-done.1
  61.3 0.3 fusion.11
  61.6 0.0 copy-start.4
  61.6 24.4 %collective-permute-done = bf16[1024,1152]{1,0:T(8,128)(2,1)} collective-permute-done((bf16[1024,1152]{1,0:T(8,128)(2,1)}, bf16[1024,1152]{1,0:T(8,128)(2,1)}, u32[]{:S(2)}, u32[]{:S(2)}) %collective-permute-start) | collective-permute-done | bytes 2359328 | tf_op jit(solution)/shard_map/ppermute | solution.py:13
  86.0 1.8 constant_dynamic-update-slice_fusion.2
  87.9 0.0 copy-done.4
  87.9 0.4 constant_dynamic-update-slice_fusion.1
  88.3 0.5 collective-permute-done.1
  88.8 0.4 constant_dynamic-update-slice_fusion
  89.2 0.0 copy-start.5
  89.2 2.9 %copy-done.5 = bf16[3072,1152]{1,0:T(8,128)(2,1)} copy-done((bf16[3072,1152]{1,0:T(8,128)(2,1)}, bf16[3072,1152]{1,0:T(8,128)(2,1)S(1)}, u32[]{:S(2)}) %copy-start.5) | copy-done | bytes 7077912
  92.1 6.1 %multiply_convert_fusion = bf16[512,3072]{1,0:T(8,128)(2,1)S(1)} fusion(bf16[3072,1152]{1,0:T(8,128)(2,1)S(1)} %constant_dynamic-update-slice_fusion, f32[]{:T(128)} %bitcast.6, s32[512]{0:T(512)S(1)} %add_add_fusion, f32[]{:T(128)} %bitcast, bf16[512,1152]{1,0:T(8,128)(2,1)S(1)} %copy-done.1, f32[512]{0:T(512)S(1)} %add_rsqrt_fusion.1), kind=kOutput, calls=%fused_computation | convolution fusion | flops 3644522496 | bytes 11407368 | tf_op jit(solution)/shard_map/dn,ln->dl/dot_general | solution.py:57
  98.2 0.0 copy-start.3
  98.3 4.5 %fusion.21 = (bf16[3072,1152]{1,0:T(8,128)(2,1)S(1)}, f32[3072,1152]{1,0:T(8,128)S(1)}) fusion(bf16[512,3072]{1,0:T(8,128)(2,1)S(1)} %multiply_convert_fusion, bf16[512,1152]{1,0:T(8,128)(2,1)S(1)} %copy-done.1, f32[512]{0:T(512)S(1)} %add_rsqrt_fusion.1), kind=kOutput, calls=%fused_computation.32 | convolution fusion | flops 3629187072 | bytes 25561088 | tf_op jit(solution)/shard_map/ij,id->jd/dot_general | solution.py:67
  102.7 0.0 copy-done.3
  102.8 0.4 fusion.20
  103.1 5.1 %collective-permute-start.2 = (bf16[1024,1152]{1,0:T(8,128)(2,1)S(1)}, bf16[1024,1152]{1,0:T(8,128)(2,1)S(1)}, u32[]{:S(2)}, u32[]{:S(2)}) collective-permute-start(bf16[1024,1152]{1,0:T(8,128)(2,1)S(1)} %get-tuple-element.2), channel_id=1, source_target_pairs={{0,254},{2,0},{4,2},{6,4},{8,6},{10,8},{12,10},{14,12},{16,14},{18... | collective-permute-start | bytes 7077896 | tf_op jit(solution)/shard_map/ppermute | solution.py:24
  108.2 0.0 collective-permute-start.3
  108.2 23.8 %collective-permute-done.2 = bf16[1024,1152]{1,0:T(8,128)(2,1)S(1)} collective-permute-done((bf16[1024,1152]{1,0:T(8,128)(2,1)S(1)}, bf16[1024,1152]{1,0:T(8,128)(2,1)S(1)}, u32[]{:S(2)}, u32[]{:S(2)}) %collective-permute-start.2) | collective-permute-done | bytes 2359328 | tf_op jit(solution)/shard_map/ppermute | solution.py:24
  132.0 2.0 collective-permute-done.3
  134.0 2.8 %fusion = f32[1024,1152]{1,0:T(8,128)} fusion(f32[3072,1152]{1,0:T(8,128)S(1)} %get-tuple-element.7, bf16[1024,1152]{1,0:T(8,128)(2,1)S(1)} %collective-permute-done.3, bf16[1024,1152]{1,0:T(8,128)(2,1)S(1)} %collective-permute-done.2), kind=kLoop, calls=%fused_computation.3 | loop fusion | flops 4718592 | bytes 14155776 | tf_op jit(solution)/shard_map/add | solution.py:76
  136.8 0.0 reduce-scatter.2.cloned.1.call-update
  136.8 8.3 %fusion.7 = (f32[512]{0:T(512)S(1)}, f32[512,1152]{1,0:T(8,128)S(1)}) fusion(bf16[512,1152]{1,0:T(8,128)(2,1)S(1)} %copy-done.1, f32[512]{0:T(512)S(1)} %add_rsqrt_fusion.1, bf16[512,3072]{1,0:T(8,128)(2,1)} %copy-done.3, bf16[3072,1152]{1,0:T(8,128)(2,1)} %copy-done.5), kind=kOutput, calls=%fused_computation.14 | convolution fusion | flops 3626237440 | bytes 13766656 | tf_op jit(solution)/shard_map/ij,jd->id/dot_general | solution.py:64
  145.2 0.0 copy-start
  145.2 1.5 fusion.10
  146.7 58.2 %reduce-scatter.2.cloned.1.call-done = f32[512,1152]{1,0:T(8,128)} async-done(((f32[1024,1152]{1,0:T(8,128)}), f32[512,1152]{1,0:T(8,128)}) %reduce-scatter.2.cloned.1.call-update) | async-done | bytes 2359312 | tf_op jit(solution)/shard_map/reduce_scatter | solution.py:77
  204.9 0.0 copy-done
  204.9 0.0 copy-start.2
  204.9 2.3 %fusion.12 = f32[512]{0:T(512)S(1)} fusion(f32[512,1152]{1,0:T(8,128)} %reduce-scatter.2.cloned.1.call-done, bf16[512,1152]{1,0:T(8,128)(2,1)S(1)} %copy-done, f32[512]{0:T(512)S(1)} %add_rsqrt_fusion), kind=kLoop, calls=%fused_computation.19 | loop fusion | flops 2358784 | bytes 3543040 | tf_op jit(solution)/shard_map/reduce_sum | solution.py:33
  207.2 0.1 copy-done.2
  207.3 1.5 fusion.15
  (3 shorter events, 0.0 us)
Async XLA Ops:
  7.2 54.1 %copy-start.1 = (bf16[512,1152]{1,0:T(8,128)(2,1)S(1)}, bf16[512,1152]{1,0:T(8,128)(2,1)}, u32[]{:S(2)}) copy-start(bf16[512,1152]{1,0:T(8,128)(2,1)} %param.4) | copy-start | bytes 3538948
  7.2 50.9 %all-gather.2.cloned.1.call-start = ((), (), s32[]{:S(2)}) async-start(), calls=%async_computation.1 | async-start | bytes 3538944 | tf_op jit(solution)/shard_map/all_gather | solution.py:51
  11.5 193.4 %reduce-scatter.2.cloned.1.call-start = ((), (), s32[]{:S(2)}) async-start(), calls=%async_computation.2 | async-start | bytes 7077888 | tf_op jit(solution)/shard_map/reduce_scatter | solution.py:77
  58.1 27.9 %collective-permute-start = (bf16[1024,1152]{1,0:T(8,128)(2,1)}, bf16[1024,1152]{1,0:T(8,128)(2,1)}, u32[]{:S(2)}, u32[]{:S(2)}) collective-permute-start(bf16[1024,1152]{1,0:T(8,128)(2,1)} %all-gather.2.cloned.1.call-done), channel_id=1, source_target_pairs={{0,2},{2,4},{4,6},{6,8},{8,10},{10,12},{12,14},{14,16},{16,18},{18... | collective-permute-start | bytes 7077896 | tf_op jit(solution)/shard_map/ppermute | solution.py:13
  59.9 28.9 %collective-permute-start.1 = (bf16[1024,1152]{1,0:T(8,128)(2,1)}, bf16[1024,1152]{1,0:T(8,128)(2,1)S(1)}, u32[]{:S(2)}, u32[]{:S(2)}) collective-permute-start(bf16[1024,1152]{1,0:T(8,128)(2,1)} %all-gather.2.cloned.1.call-done), channel_id=1, source_target_pairs={{2,0},{4,2},{6,4},{8,6},{10,8},{12,10},{14,12},{16,14},{18,16},{20... | collective-permute-start | bytes 7077896 | tf_op jit(solution)/shard_map/ppermute | solution.py:16
  61.6 26.3 %copy-start.4 = (bf16[1024,1152]{1,0:T(8,128)(2,1)S(1)}, bf16[1024,1152]{1,0:T(8,128)(2,1)}, u32[]{:S(2)}) copy-start(bf16[1024,1152]{1,0:T(8,128)(2,1)} %all-gather.2.cloned.1.call-done) | copy-start | bytes 7077892
  89.2 2.9 %copy-start.5 = (bf16[3072,1152]{1,0:T(8,128)(2,1)}, bf16[3072,1152]{1,0:T(8,128)(2,1)S(1)}, u32[]{:S(2)}) copy-start(bf16[3072,1152]{1,0:T(8,128)(2,1)S(1)} %constant_dynamic-update-slice_fusion) | copy-start | bytes 21233668
  98.2 4.5 %copy-start.3 = (bf16[512,3072]{1,0:T(8,128)(2,1)}, bf16[512,3072]{1,0:T(8,128)(2,1)S(1)}, u32[]{:S(2)}) copy-start(bf16[512,3072]{1,0:T(8,128)(2,1)S(1)} %multiply_convert_fusion) | copy-start | bytes 9437188
  103.1 28.8 %collective-permute-start.2 = (bf16[1024,1152]{1,0:T(8,128)(2,1)S(1)}, bf16[1024,1152]{1,0:T(8,128)(2,1)S(1)}, u32[]{:S(2)}, u32[]{:S(2)}) collective-permute-start(bf16[1024,1152]{1,0:T(8,128)(2,1)S(1)} %get-tuple-element.2), channel_id=1, source_target_pairs={{0,254},{2,0},{4,2},{6,4},{8,6},{10,8},{12,10},{14,12},{16,14},{18... | collective-permute-start | bytes 7077896 | tf_op jit(solution)/shard_map/ppermute | solution.py:24
  108.2 25.8 %collective-permute-start.3 = (bf16[1024,1152]{1,0:T(8,128)(2,1)S(1)}, bf16[1024,1152]{1,0:T(8,128)(2,1)S(1)}, u32[]{:S(2)}, u32[]{:S(2)}) collective-permute-start(bf16[1024,1152]{1,0:T(8,128)(2,1)S(1)} %get-tuple-element.3), channel_id=1, source_target_pairs={{0,2},{2,4},{4,6},{6,8},{8,10},{10,12},{12,14},{14,16},{16,18},{18... | collective-permute-start | bytes 7077896 | tf_op jit(solution)/shard_map/ppermute | solution.py:24
  145.2 59.7 %copy-start = (bf16[512,1152]{1,0:T(8,128)(2,1)S(1)}, bf16[512,1152]{1,0:T(8,128)(2,1)}, u32[]{:S(2)}) copy-start(bf16[512,1152]{1,0:T(8,128)(2,1)} %param.5) | copy-start | bytes 3538948
  204.9 2.4 %copy-start.2 = (f32[512,1152]{1,0:T(8,128)S(1)}, f32[512,1152]{1,0:T(8,128)}, u32[]{:S(2)}) copy-start(f32[512,1152]{1,0:T(8,128)} %reduce-scatter.2.cloned.1.call-done) | copy-start | bytes 7077892
Sparse Core Ops, SparseCore 0:
  11.6 46.4 all-gather.1
  137.0 67.8 reduce-scatter.1
where the time goes:
time: 216 us
  waiting for transfers between devices  156 us (72%)
  matrix products  18.9 us (9%)
  between operations  15.5 us (7%)
  other arithmetic  12.6 us (6%)
  starting transfers between devices  7 us (3%)
  local copies, waits for them, and re-layouts  5.96 us (3%)
    reduce_scatter x1, waiting for transfers between devices, shards(): lax.psum_scatter(caption_terms, 'rep', scatter_dimension=0, tiled=True)  58.2 us
    all_gather x1, waiting for transfers between devices, shards(): lax.all_gather(caption_unit, 'rep', axis=0, tiled=True)  46.6 us
    ppermute x2, waiting for transfers between devices, shifted(): return lax.ppermute(value, axis, pairs)  25.8 us
    ppermute x1, waiting for transfers between devices, padded(): lax.ppermute(lax.slice_in_dim(block, block.shape[dim] - width, None, axis...  24.4 us
    dot_general x1, matrix products, shards(): jnp.einsum('ij,jd->id', logistic_factor, window, preferred_element_type=j...  8.32 us
    dot_general x1, matrix products, shards(): jnp.einsum('dn,ln->dl', image_unit, window, preferred_element_type=jnp.fl...  6.14 us
    unnamed x14, local copies, waits for them, and re-layouts  5.24 us
    ppermute x2, starting transfers between devices, shifted(): return lax.ppermute(value, axis, pairs)  5.08 us
  transfers between devices with their start and end apart: 6, of which 6 were waited for; matrix products, arithmetic and copies ran while one was open for 6% of the time, Pallas kernels for 0%

commit v1 on v0

v1 whole, which is shorter than its diff:
```python
import functools

import jax
import jax.numpy as jnp
from jax import lax
from jax.experimental import pallas as pl
from jax.experimental.pallas import tpu as pltpu
from jax.sharding import PartitionSpec as P

MESH = pl.DeviceIdType.MESH
PIECES = 8
SHIFTED = 0
AHEAD = 8
OUT_NEAR, REP, IN_FAR, OUT_FAR = range(4)


def kernel(
    n_blk, n_z, exp_ref, icpt_ref, img_hbm, cap_hbm, gi_hbm, gc_hbm,
    raw, inv, own, pdir, win, acc, res,
    raw_sem, out_sem, win_recv, pdir_recv, rep_send, out_send, in_send, fin_send, fout_send, e_send, e2_send,
):
    rows, width = own.shape[1], own.shape[2]
    pr = rows // PIECES
    blk, rep = lax.axis_index("blk"), lax.axis_index("rep")
    core = lax.rem(blk, 2)
    z = lax.rem(blk // 2, n_z)
    away = 2 * core - 1
    outer = lax.rem(blk + away + n_blk, n_blk)
    inner = blk - away
    z_end = core * (n_z - 1)
    edge = z == z_end
    behind = (core == 0) & (z == n_z - 1) | (core == 1) & (z == 0)
    beside = (core == 1) & (z == n_z - 2) | (core == 0) & (z == 1)
    rep_id = {"blk": blk, "rep": 1 - rep}
    inner_id = {"blk": inner, "rep": rep}
    outer_id = {"blk": outer, "rep": rep}
    cross_id = {"blk": outer, "rep": 1 - rep}

    def rows_of(j):
        return pl.ds(pl.multiple_of(j * pr, pr), pr)

    def load(j):
        return (
            pltpu.make_async_copy(cap_hbm.at[rows_of(j)], raw.at[0, rows_of(j)], raw_sem.at[0, j]),
            pltpu.make_async_copy(img_hbm.at[rows_of(j)], raw.at[1, rows_of(j)], raw_sem.at[1, j]),
        )

    def slot(place, j):
        return win.at[j, :, pl.ds(place * pr, pr)]

    def remote(src, dst, send, recv, target):
        return pltpu.make_async_remote_copy(
            src_ref=src, dst_ref=dst, send_sem=send, recv_sem=recv, device_id=target, device_id_type=MESH
        )

    def mine(j):
        return own.at[:, rows_of(j)]

    def to_rep(j):
        return remote(mine(j), slot(REP, j), rep_send.at[j], win_recv.at[REP, j], rep_id)

    def to_outer(j):
        return remote(mine(j), slot(OUT_NEAR, j), out_send.at[j], win_recv.at[OUT_NEAR, j], outer_id)

    def to_inner(j):
        return remote(mine(j), pdir.at[:, rows_of(j)], in_send.at[j], pdir_recv.at[j], inner_id)

    def to_cross(j):
        return remote(mine(j), slot(OUT_FAR, j), fout_send.at[j], win_recv.at[OUT_FAR, j], cross_id)

    def pass_inner(j):
        return remote(slot(REP, j), slot(IN_FAR, j), fin_send.at[j], win_recv.at[IN_FAR, j], inner_id)

    def pass_outer(j):
        return remote(slot(REP, j), slot(OUT_FAR, j), fout_send.at[j], win_recv.at[OUT_FAR, j], outer_id)

    def pass_rep(j):
        return remote(slot(OUT_NEAR, j), slot(OUT_FAR, j), e_send.at[j], win_recv.at[OUT_FAR, j], rep_id)

    def pass_back(j):
        return remote(slot(OUT_FAR, j), slot(REP, j), e2_send.at[j], win_recv.at[REP, j], outer_id)

    def got(place, j):
        pltpu.make_async_copy(slot(place, j), slot(place, j), win_recv.at[place, j]).wait()

    def each(count, body):
        lax.fori_loop(0, count, lambda j, c: (body(j), c)[1], 0)

    each(PIECES, lambda j: [c.start() for c in load(j)])

    barrier = pltpu.get_barrier_semaphore()
    for target in (rep_id, inner_id, outer_id, cross_id):
        pl.semaphore_signal(barrier, inc=1, device_id=target, device_id_type=MESH)
    pl.semaphore_wait(barrier, 4)

    def send_mine(j):
        @pl.when(jnp.logical_not(behind & (j < SHIFTED)))
        def _():
            to_rep(j).start()

        to_outer(j).start()
        to_inner(j).start()

        @pl.when(edge)
        def _():
            to_cross(j).start()

    def prepare(j):
        for c in load(j):
            c.wait()
        for a in range(2):
            values = raw[a, rows_of(j), :].astype(jnp.float32)
            inverse = lax.rsqrt(jnp.sum(values * values, axis=1, keepdims=True) + 1e-06)
            own[a, rows_of(j), :] = (values * inverse).astype(jnp.bfloat16)
            inv[a, rows_of(j), :] = inverse

        @pl.when(j < AHEAD)
        def _():
            send_mine(j)

    each(PIECES, prepare)

    scale = jnp.exp(exp_ref[...])
    icpt = icpt_ref[...]

    def weights(side, others, diagonal):
        product = lax.dot_general(
            own[side], others, (((1,), (1,)), ((), ())), preferred_element_type=jnp.float32
        )
        logits = scale * product + icpt
        if diagonal is None:
            factor = scale / (1.0 + jnp.exp(-logits))
        else:
            row = lax.broadcasted_iota(jnp.int32, product.shape, 0)
            col = lax.broadcasted_iota(jnp.int32, product.shape, 1) + diagonal
            agree = row == col
            factor = jnp.where(agree, -scale, scale) / (1.0 + jnp.exp(jnp.where(agree, logits, -logits)))
        return factor.astype(jnp.bfloat16)

    def step(caps, imgs, diagonal=None, first=False):
        for side, others in ((1, caps), (0, imgs)):
            term = lax.dot_general(
                weights(side, others, diagonal), others, (((1,), (0,)), ((), ())),
                preferred_element_type=jnp.float32,
            )
            acc[side] = term if first else acc[side] + term

    half = rows // 2
    step(own[0, :half], own[1, :half], 0, True)
    step(own[0, half:], own[1, half:], half)

    each(PIECES, lambda j: pltpu.make_async_copy(
        pdir.at[:, rows_of(j)], pdir.at[:, rows_of(j)], pdir_recv.at[j]).wait())

    def inner_step(k):
        at = pl.ds(pl.multiple_of(k * half, half), half)
        step(pdir[0, at, :], pdir[1, at, :])

    each(2, inner_step)

    def serve(j):
        got(REP, j)
        pass_inner(j).start()

        @pl.when(jnp.logical_not(edge | behind & (j < SHIFTED)))
        def _():
            pass_outer(j).start()

        got(OUT_NEAR, j)

        @pl.when(beside & (j < SHIFTED))
        def _():
            pass_rep(j).start()

        @pl.when(j + AHEAD < PIECES)
        def _():
            send_mine(j + AHEAD)

    def finish(j):
        got(OUT_FAR, j)

        @pl.when(beside & (j < SHIFTED))
        def _():
            pass_back(j).start()

        got(IN_FAR, j)
        step(win[j, 0], win[j, 1])

    serve(0)

    def body(j):
        @pl.when(j < PIECES)
        def _():
            serve(j)
        finish(j - 1)

    lax.fori_loop(1, PIECES + 1, lambda j, c: (body(j), c)[1], 0)

    def close(a, out):
        def part(j):
            direction = raw[a, rows_of(j), :].astype(jnp.float32) * inv[a, rows_of(j), :]
            upstream = acc[a, rows_of(j), :]
            along = jnp.sum(upstream * direction, axis=1, keepdims=True)
            res[a, rows_of(j), :] = (inv[a, rows_of(j), :] * (upstream - direction * along)).astype(jnp.bfloat16)
            pltpu.make_async_copy(res.at[a, rows_of(j)], out.at[rows_of(j)], out_sem.at[a, j]).start()
        each(PIECES, part)

    close(1, gi_hbm)
    close(0, gc_hbm)

    def drain(j):
        for a, out in ((1, gi_hbm), (0, gc_hbm)):
            pltpu.make_async_copy(res.at[a, rows_of(j)], out.at[rows_of(j)], out_sem.at[a, j]).wait()
        to_outer(j).wait_send()
        to_inner(j).wait_send()
        pass_inner(j).wait_send()

        @pl.when(jnp.logical_not(behind & (j < SHIFTED)))
        def _():
            to_rep(j).wait_send()

        @pl.when(edge)
        def _():
            to_cross(j).wait_send()

        @pl.when(jnp.logical_not(edge | behind & (j < SHIFTED)))
        def _():
            pass_outer(j).wait_send()

        @pl.when(beside & (j < SHIFTED))
        def _():
            pass_rep(j).wait_send()
            pass_back(j).wait_send()

    each(PIECES, drain)


def solution(mesh):
    n_blk = mesh.shape["blk"]

    def shards(photo_vectors, caption_vectors, exponent_of_scale, additive_intercept):
        rows, width = photo_vectors.shape
        pr = rows // PIECES
        bf16, f32 = jnp.bfloat16, jnp.float32
        dma = pltpu.SemaphoreType.DMA
        vmem = pl.BlockSpec(memory_space=pltpu.VMEM)
        anywhere = pl.BlockSpec(memory_space=pl.ANY)
        return pl.pallas_call(
            functools.partial(kernel, n_blk, 8),
            out_shape=[jax.ShapeDtypeStruct((rows, width), bf16)] * 2,
            in_specs=[vmem, vmem, anywhere, anywhere],
            out_specs=[anywhere] * 2,
            scratch_shapes=[
                pltpu.VMEM((2, rows, width), bf16),
                pltpu.VMEM((2, rows, 1), f32),
                pltpu.VMEM((2, rows, width), bf16),
                pltpu.VMEM((2, rows, width), bf16),
                pltpu.VMEM((PIECES, 2, 4 * pr, width), bf16),
                pltpu.VMEM((2, rows, width), f32),
                pltpu.VMEM((2, rows, width), bf16),
                dma((2, PIECES)),
                dma((2, PIECES)),
                dma((4, PIECES)),
            ] + [dma((PIECES,))] * 8,
            compiler_params=pltpu.CompilerParams(
                collective_id=0, has_side_effects=True, vmem_limit_bytes=56 * 1024 * 1024
            ),
            cost_estimate=pl.CostEstimate(
                flops=24 * 2 * rows * rows * width, bytes_accessed=8 * rows * width, transcendentals=12 * rows * rows
            ),
        )(
            exponent_of_scale.reshape(1, 1), additive_intercept.reshape(1, 1), photo_vectors, caption_vectors
        )

    whole = P(("blk", "rep"), None)
    return jax.shard_map(
        shards,
        mesh=mesh,
        in_specs=(whole, whole, P(), P()),
        out_specs=(whole, whole),
        check_vma=False,
    )
```

time: 216 us -> 105 us (0.49)
  the two profiles are of different devices: /device:TPU:1 before, /device:TPU:20 now
where the time goes in v1:
time: 105 us
  Pallas kernels  99.6 us (95%)
  local copies, waits for them, and re-layouts  3.49 us (3%)
  between operations  1.94 us (2%)
    pallas_call x1, Pallas kernels, shards(): pl.pallas_call(functools.partial(kernel, n_blk, 8), out_shape=[jax.ShapeD...  99.6 us
    unnamed x4, local copies, waits for them, and re-layouts  3.49 us

profile of v1, /device:TPU:20, one launch (start us, length us, event | category | flops | bytes accessed | tf_op | source)
XLA Modules:
  0.0 105.0 jit_solution(1894605432645581408)
XLA Ops:
  1.9 99.6 %shard_map.59 = (bf16[512,1152]{1,0:T(8,128)(2,1)}, bf16[512,1152]{1,0:T(8,128)(2,1)}) custom-call(f32[1,1]{1,0:T(1,128)} %bitcast.2.exp_ref, f32[1,1]{1,0:T(1,128)} %bitcast.3.icpt_ref, bf16[512,1152]{1,0:T(8,128)(2,1)} %img_hbm.1, bf16[512,1152]{1,0:T(8,128)(2,1)} %cap_hbm.1), custom_call_target="tpu_custom_call" | custom-call | flops 14495514624 | bytes 4718592 | tf_op jit(solution)/shard_map/pallas_call | solution.py:248
  101.5 0.0 copy-start
  101.5 2.5 %copy.10 = bf16[512,1152]{1,0:T(8,128)(2,1)} copy(bf16[512,1152]{1,0:T(8,128)(2,1)} %get-tuple-element.4) | data formatting | bytes 2359296
  104.0 0.0 copy-done
  104.0 1.0 copy.11
Async XLA Ops:
  101.5 2.5 %copy-start = (bf16[512,1152]{1,0:T(8,128)(2,1)S(1)}, bf16[512,1152]{1,0:T(8,128)(2,1)}, u32[]{:S(2)}) copy-start(bf16[512,1152]{1,0:T(8,128)(2,1)} %get-tuple-element.5) | copy-start | bytes 3538948

commit v2 on v1

--- a/solution.py
+++ b/solution.py
@@ -9,15 +9,17 @@
 
 MESH = pl.DeviceIdType.MESH
 PIECES = 8
-SHIFTED = 0
-AHEAD = 8
+SEND_AHEAD = 4
+RELAY_AHEAD = 2
+EXTRA = 0
 OUT_NEAR, REP, IN_FAR, OUT_FAR = range(4)
 
 
 def kernel(
     n_blk, n_z, exp_ref, icpt_ref, img_hbm, cap_hbm, gi_hbm, gc_hbm,
-    raw, inv, own, pdir, win, acc, res,
-    raw_sem, out_sem, win_recv, pdir_recv, rep_send, out_send, in_send, fin_send, fout_send, e_send, e2_send,
+    raw, inv, own, pdir, win, relay, acc, res,
+    raw_sem, out_sem, win_recv, pdir_recv, relay_recv,
+    in_send, rep_send, out_send, fin_send, fout_send, near_send, far_send, cross_send,
 ):
     rows, width = own.shape[1], own.shape[2]
     pr = rows // PIECES
@@ -27,14 +29,19 @@
     away = 2 * core - 1
     outer = lax.rem(blk + away + n_blk, n_blk)
     inner = blk - away
-    z_end = core * (n_z - 1)
-    edge = z == z_end
-    behind = (core == 0) & (z == n_z - 1) | (core == 1) & (z == 0)
-    beside = (core == 1) & (z == n_z - 2) | (core == 0) & (z == 1)
+    edge = z == core * (n_z - 1)
+    inside = jnp.logical_not(edge)
+    pal = blk + 2 * n_z * (1 - 2 * lax.rem(blk // (2 * n_z), 2))
+    beyond = lax.rem(pal + away + n_blk, n_blk)
+    outer_low = lax.rem(outer // (2 * n_z), 2)
+    source = outer + 2 * n_z * (1 - 2 * outer_low)
     rep_id = {"blk": blk, "rep": 1 - rep}
     inner_id = {"blk": inner, "rep": rep}
     outer_id = {"blk": outer, "rep": rep}
-    cross_id = {"blk": outer, "rep": 1 - rep}
+    near_id = {"blk": pal, "rep": rep}
+    far_id = {"blk": pal, "rep": 1 - rep}
+    beyond_id = {"blk": beyond, "rep": rep}
+    source_id = {"blk": source, "rep": rep}
 
     def rows_of(j):
         return pl.ds(pl.multiple_of(j * pr, pr), pr)
@@ -65,8 +72,11 @@
     def to_inner(j):
         return remote(mine(j), pdir.at[:, rows_of(j)], in_send.at[j], pdir_recv.at[j], inner_id)
 
-    def to_cross(j):
-        return remote(mine(j), slot(OUT_FAR, j), fout_send.at[j], win_recv.at[OUT_FAR, j], cross_id)
+    def to_near(j):
+        return remote(mine(j), relay.at[0, :, rows_of(j)], rep_send.at[j], relay_recv.at[0, j], near_id)
+
+    def to_far(j):
+        return remote(mine(j), relay.at[1, :, rows_of(j)], out_send.at[j], relay_recv.at[1, j], far_id)
 
     def pass_inner(j):
         return remote(slot(REP, j), slot(IN_FAR, j), fin_send.at[j], win_recv.at[IN_FAR, j], inner_id)
@@ -74,36 +84,45 @@
     def pass_outer(j):
         return remote(slot(REP, j), slot(OUT_FAR, j), fout_send.at[j], win_recv.at[OUT_FAR, j], outer_id)
 
-    def pass_rep(j):
-        return remote(slot(OUT_NEAR, j), slot(OUT_FAR, j), e_send.at[j], win_recv.at[OUT_FAR, j], rep_id)
-
-    def pass_back(j):
-        return remote(slot(OUT_FAR, j), slot(REP, j), e2_send.at[j], win_recv.at[REP, j], outer_id)
+    def near_beyond(j):
+        return remote(relay.at[0, :, rows_of(j)], slot(OUT_NEAR, j), near_send.at[j], win_recv.at[OUT_NEAR, j], beyond_id)
+
+    def far_beyond(j):
+        return remote(relay.at[1, :, rows_of(j)], slot(OUT_FAR, j), far_send.at[j], win_recv.at[OUT_FAR, j], beyond_id)
+
+    def near_across(j):
+        return remote(relay.at[0, :, rows_of(j)], slot(REP, j), cross_send.at[0, j], win_recv.at[REP, j], far_id)
+
+    def far_across(j):
+        return remote(relay.at[1, :, rows_of(j)], slot(REP, j), cross_send.at[1, j], win_recv.at[REP, j], near_id)
 
     def got(place, j):
         pltpu.make_async_copy(slot(place, j), slot(place, j), win_recv.at[place, j]).wait()
 
+    def got_relay(side, j):
+        at = relay.at[side, :, rows_of(j)]
+        pltpu.make_async_copy(at, at, relay_recv.at[side, j]).wait()
+
     def each(count, body):
         lax.fori_loop(0, count, lambda j, c: (body(j), c)[1], 0)
 
     each(PIECES, lambda j: [c.start() for c in load(j)])
 
     barrier = pltpu.get_barrier_semaphore()
-    for target in (rep_id, inner_id, outer_id, cross_id):
-        pl.semaphore_signal(barrier, inc=1, device_id=target, device_id_type=MESH)
-    pl.semaphore_wait(barrier, 4)
-
-    def send_mine(j):
-        @pl.when(jnp.logical_not(behind & (j < SHIFTED)))
-        def _():
-            to_rep(j).start()
-
-        to_outer(j).start()
-        to_inner(j).start()
-
-        @pl.when(edge)
-        def _():
-            to_cross(j).start()
+
+    def greet(*targets):
+        for target in targets:
+            pl.semaphore_signal(barrier, inc=1, device_id=target, device_id_type=MESH)
+
+    greet(inner_id)
+
+    @pl.when(inside)
+    def _():
+        greet(rep_id, outer_id)
+
+    @pl.when(edge)
+    def _():
+        greet(near_id, far_id, beyond_id, source_id)
 
     def prepare(j):
         for c in load(j):
@@ -114,11 +133,47 @@
             own[a, rows_of(j), :] = (values * inverse).astype(jnp.bfloat16)
             inv[a, rows_of(j), :] = inverse
 
-        @pl.when(j < AHEAD)
-        def _():
-            send_mine(j)
-
-    each(PIECES, prepare)
+    def send_first(j):
+        @pl.when(inside)
+        def _():
+            to_rep(j).start()
+
+        @pl.when(edge)
+        def _():
+            to_near(j).start()
+
+    def send_second(j):
+        @pl.when(inside)
+        def _():
+            to_outer(j).start()
+
+        @pl.when(edge)
+        def _():
+            to_far(j).start()
+
+    prepare(0)
+
+    @pl.when(inside)
+    def _():
+        pl.semaphore_wait(barrier, 3)
+
+    @pl.when(edge)
+    def _():
+        pl.semaphore_wait(barrier, 5)
+
+    def begin(j):
+        @pl.when(j > 0)
+        def _():
+            prepare(j)
+
+        @pl.when(j < SEND_AHEAD)
+        def _():
+            send_first(j)
+            send_second(j)
+
+        to_inner(j).start()
+
+    each(PIECES, begin)
 
     scale = jnp.exp(exp_ref[...])
     icpt = icpt_ref[...]
@@ -138,63 +193,78 @@
         return factor.astype(jnp.bfloat16)
 
     def step(caps, imgs, diagonal=None, first=False):
-        for side, others in ((1, caps), (0, imgs)):
-            term = lax.dot_general(
-                weights(side, others, diagonal), others, (((1,), (0,)), ((), ())),
-                preferred_element_type=jnp.float32,
-            )
+        factors = [weights(1, caps, diagonal), weights(0, imgs, diagonal)]
+        for side, others, factor in ((1, caps, factors[0]), (0, imgs, factors[1])):
+            term = lax.dot_general(factor, others, (((1,), (0,)), ((), ())), preferred_element_type=jnp.float32)
             acc[side] = term if first else acc[side] + term
 
+    def hand_on(j):
+        @pl.when(edge)
+        def _():
+            turn = lax.rem(j, 2) == rep
+            got_relay(0, j)
+
+            @pl.when(turn)
+            def _():
+                near_across(j).start()
+
+            near_beyond(j).start()
+            got_relay(1, j)
+
+            @pl.when(turn)
+            def _():
+                far_across(j).start()
+
+            far_beyond(j).start()
+
+    def serve(j):
+        @pl.when(j + SEND_AHEAD < PIECES)
+        def _():
+            send_first(j + SEND_AHEAD)
+            send_second(j + SEND_AHEAD)
+
+        @pl.when(j + RELAY_AHEAD < PIECES)
+        def _():
+            hand_on(j + RELAY_AHEAD)
+
+        got(REP, j)
+        pass_inner(j).start()
+
+        @pl.when(inside)
+        def _():
+            pass_outer(j).start()
+
+    def finish(j):
+        got(OUT_NEAR, j)
+        got(OUT_FAR, j)
+        got(IN_FAR, j)
+        step(win[j, 0], win[j, 1])
+
     half = rows // 2
-    step(own[0, :half], own[1, :half], 0, True)
-    step(own[0, half:], own[1, half:], half)
+    for k in range(RELAY_AHEAD):
+        hand_on(k)
+        if k < 2:
+            step(own[0, k * half:(k + 1) * half], own[1, k * half:(k + 1) * half], k * half, k == 0)
 
     each(PIECES, lambda j: pltpu.make_async_copy(
         pdir.at[:, rows_of(j)], pdir.at[:, rows_of(j)], pdir_recv.at[j]).wait())
 
-    def inner_step(k):
-        at = pl.ds(pl.multiple_of(k * half, half), half)
-        step(pdir[0, at, :], pdir[1, at, :])
-
-    each(2, inner_step)
-
-    def serve(j):
-        got(REP, j)
-        pass_inner(j).start()
-
-        @pl.when(jnp.logical_not(edge | behind & (j < SHIFTED)))
-        def _():
-            pass_outer(j).start()
-
-        got(OUT_NEAR, j)
-
-        @pl.when(beside & (j < SHIFTED))
-        def _():
-            pass_rep(j).start()
-
-        @pl.when(j + AHEAD < PIECES)
-        def _():
-            send_mine(j + AHEAD)
-
-    def finish(j):
-        got(OUT_FAR, j)
-
-        @pl.when(beside & (j < SHIFTED))
-        def _():
-            pass_back(j).start()
-
-        got(IN_FAR, j)
-        step(win[j, 0], win[j, 1])
-
-    serve(0)
-
     def body(j):
         @pl.when(j < PIECES)
         def _():
             serve(j)
-        finish(j - 1)
-
-    lax.fori_loop(1, PIECES + 1, lambda j, c: (body(j), c)[1], 0)
+
+        @pl.when(j < 2)
+        def _():
+            at = pl.ds(pl.multiple_of(j * half, half), half)
+            step(pdir[0, at, :], pdir[1, at, :])
+
+        @pl.when(j > 0)
+        def _():
+            finish(j - 1)
+
+    each(PIECES + 1, body)
+    each(EXTRA, lambda j: step(win[j, 0], win[j, 1]))
 
     def close(a, out):
         def part(j):
@@ -211,26 +281,26 @@
     def drain(j):
         for a, out in ((1, gi_hbm), (0, gc_hbm)):
             pltpu.make_async_copy(res.at[a, rows_of(j)], out.at[rows_of(j)], out_sem.at[a, j]).wait()
-        to_outer(j).wait_send()
         to_inner(j).wait_send()
         pass_inner(j).wait_send()
 
-        @pl.when(jnp.logical_not(behind & (j < SHIFTED)))
+        @pl.when(inside)
         def _():
             to_rep(j).wait_send()
+            to_outer(j).wait_send()
+            pass_outer(j).wait_send()
 
         @pl.when(edge)
         def _():
-            to_cross(j).wait_send()
-
-        @pl.when(jnp.logical_not(edge | behind & (j < SHIFTED)))
-        def _():
-            pass_outer(j).wait_send()
-
-        @pl.when(beside & (j < SHIFTED))
-        def _():
-            pass_rep(j).wait_send()
-            pass_back(j).wait_send()
+            to_near(j).wait_send()
+            to_far(j).wait_send()
+            near_beyond(j).wait_send()
+            far_beyond(j).wait_send()
+
+            @pl.when(lax.rem(j, 2) == rep)
+            def _():
+                near_across(j).wait_send()
+                far_across(j).wait_send()
 
     each(PIECES, drain)
 
@@ -256,12 +326,15 @@
                 pltpu.VMEM((2, rows, width), bf16),
                 pltpu.VMEM((2, rows, width), bf16),
                 pltpu.VMEM((PIECES, 2, 4 * pr, width), bf16),
+                pltpu.VMEM((2, 2, rows, width), bf16),
                 pltpu.VMEM((2, rows, width), f32),
                 pltpu.VMEM((2, rows, width), bf16),
                 dma((2, PIECES)),
                 dma((2, PIECES)),
                 dma((4, PIECES)),
-            ] + [dma((PIECES,))] * 8,
+                dma((PIECES,)),
+                dma((2, PIECES)),
+            ] + [dma((PIECES,))] * 7 + [dma((2, PIECES))],
             compiler_params=pltpu.CompilerParams(
                 collective_id=0, has_side_effects=True, vmem_limit_bytes=56 * 1024 * 1024
             ),

time: 105 us -> 91.6 us (0.87)
  the two profiles are of different devices: /device:TPU:20 before, /device:TPU:8 now
where the time goes in v2:
time: 91.6 us; the launch traced here: 91.5 us
  Pallas kernels  86.1 us (94%)
  local copies, waits for them, and re-layouts  3.49 us (4%)
  between operations  1.94 us (2%)
    pallas_call x1, Pallas kernels, shards(): pl.pallas_call(functools.partial(kernel, n_blk, 8), out_shape=[jax.ShapeD...  86.1 us
    unnamed x4, local copies, waits for them, and re-layouts  3.49 us

profile of v2, /device:TPU:8, one launch (start us, length us, event | category | flops | bytes accessed | tf_op | source)
XLA Modules:
  0.0 91.5 jit_solution(8307130482645419802)
XLA Ops:
  1.9 86.1 %shard_map.59 = (bf16[512,1152]{1,0:T(8,128)(2,1)}, bf16[512,1152]{1,0:T(8,128)(2,1)}) custom-call(f32[1,1]{1,0:T(1,128)} %bitcast.2.exp_ref, f32[1,1]{1,0:T(1,128)} %bitcast.3.icpt_ref, bf16[512,1152]{1,0:T(8,128)(2,1)} %img_hbm.1, bf16[512,1152]{1,0:T(8,128)(2,1)} %cap_hbm.1), custom_call_target="tpu_custom_call" | custom-call | flops 14495514624 | bytes 4718592 | tf_op jit(solution)/shard_map/pallas_call | solution.py:318
  88.0 0.0 copy-start
  88.0 2.5 %copy.10 = bf16[512,1152]{1,0:T(8,128)(2,1)} copy(bf16[512,1152]{1,0:T(8,128)(2,1)} %get-tuple-element.4) | data formatting | bytes 2359296
  90.5 0.0 copy-done
  90.5 1.0 %copy.11 = bf16[512,1152]{1,0:T(8,128)(2,1)} copy(bf16[512,1152]{1,0:T(8,128)(2,1)S(1)} %copy-done) | data formatting | bytes 2359296
Async XLA Ops:
  88.0 2.5 %copy-start = (bf16[512,1152]{1,0:T(8,128)(2,1)S(1)}, bf16[512,1152]{1,0:T(8,128)(2,1)}, u32[]{:S(2)}) copy-start(bf16[512,1152]{1,0:T(8,128)(2,1)} %get-tuple-element.5) | copy-start | bytes 3538948

commit v3 on v2

--- a/solution.py
+++ b/solution.py
@@ -11,7 +11,11 @@
 PIECES = 8
 SEND_AHEAD = 4
 RELAY_AHEAD = 2
-EXTRA = 0
+SHIFTED = 2
+SHIFT_OUT = 1
+SHIFT_BACK = 3
+PREPARE = 2
+CLOSE = 256
 OUT_NEAR, REP, IN_FAR, OUT_FAR = range(4)
 
 
@@ -19,7 +23,7 @@
     n_blk, n_z, exp_ref, icpt_ref, img_hbm, cap_hbm, gi_hbm, gc_hbm,
     raw, inv, own, pdir, win, relay, acc, res,
     raw_sem, out_sem, win_recv, pdir_recv, relay_recv,
-    in_send, rep_send, out_send, fin_send, fout_send, near_send, far_send, cross_send,
+    in_send, rep_send, out_send, fin_send, fout_send, near_send, far_send, cross_send, shift_send, back_send,
 ):
     rows, width = own.shape[1], own.shape[2]
     pr = rows // PIECES
@@ -31,6 +35,8 @@
     inner = blk - away
     edge = z == core * (n_z - 1)
     inside = jnp.logical_not(edge)
+    behind = z == (1 - core) * (n_z - 1)
+    beside = z == core * (n_z - 2) + (1 - core)
     pal = blk + 2 * n_z * (1 - 2 * lax.rem(blk // (2 * n_z), 2))
     beyond = lax.rem(pal + away + n_blk, n_blk)
     outer_low = lax.rem(outer // (2 * n_z), 2)
@@ -84,6 +90,12 @@
     def pass_outer(j):
         return remote(slot(REP, j), slot(OUT_FAR, j), fout_send.at[j], win_recv.at[OUT_FAR, j], outer_id)
 
+    def shift_rep(j):
+        return remote(slot(OUT_NEAR, j), slot(OUT_FAR, j), shift_send.at[j], win_recv.at[OUT_FAR, j], rep_id)
+
+    def shift_back(j):
+        return remote(slot(OUT_FAR, j), slot(REP, j), back_send.at[j], win_recv.at[REP, j], outer_id)
+
     def near_beyond(j):
         return remote(relay.at[0, :, rows_of(j)], slot(OUT_NEAR, j), near_send.at[j], win_recv.at[OUT_NEAR, j], beyond_id)
 
@@ -124,17 +136,22 @@
     def _():
         greet(near_id, far_id, beyond_id, source_id)
 
-    def prepare(j):
-        for c in load(j):
-            c.wait()
+    def prepare(part):
+        for k in range(PREPARE):
+            for c in load(part * PREPARE + k):
+                c.wait()
+        at = pl.ds(pl.multiple_of(part * PREPARE * pr, PREPARE * pr), PREPARE * pr)
         for a in range(2):
-            values = raw[a, rows_of(j), :].astype(jnp.float32)
+            values = raw[a, at, :].astype(jnp.float32)
             inverse = lax.rsqrt(jnp.sum(values * values, axis=1, keepdims=True) + 1e-06)
-            own[a, rows_of(j), :] = (values * inverse).astype(jnp.bfloat16)
-            inv[a, rows_of(j), :] = inverse
+            own[a, at, :] = (values * inverse).astype(jnp.bfloat16)
+            inv[a, at, :] = inverse
+
+    def stays(j):
+        return inside & jnp.logical_not(behind & (j >= PIECES - SHIFTED))
 
     def send_first(j):
-        @pl.when(inside)
+        @pl.when(stays(j))
         def _():
             to_rep(j).start()
 
@@ -143,7 +160,7 @@
             to_near(j).start()
 
     def send_second(j):
-        @pl.when(inside)
+        @pl.when(stays(j))
         def _():
             to_outer(j).start()
 
@@ -161,22 +178,32 @@
     def _():
         pl.semaphore_wait(barrier, 5)
 
-    def begin(j):
-        @pl.when(j > 0)
-        def _():
-            prepare(j)
-
-        @pl.when(j < SEND_AHEAD)
-        def _():
-            send_first(j)
-            send_second(j)
-
-        to_inner(j).start()
-
-    each(PIECES, begin)
-
-    scale = jnp.exp(exp_ref[...])
-    icpt = icpt_ref[...]
+    def begin(part):
+        @pl.when(part > 0)
+        def _():
+            prepare(part)
+
+        for k in range(PREPARE):
+            j = part * PREPARE + k
+
+            @pl.when(j < SEND_AHEAD)
+            def _():
+                send_first(j)
+                send_second(j)
+
+            to_inner(j).start()
+
+    each(PIECES // PREPARE, begin)
+
+    def shifted(body):
+        lax.fori_loop(PIECES - SHIFTED, PIECES, lambda j, c: (body(j), c)[1], 0)
+
+    @pl.when(behind)
+    def _():
+        shifted(lambda j: to_outer(j).start())
+
+    scale = jnp.exp(jnp.full((1, 1), exp_ref[0], jnp.float32))
+    icpt = jnp.full((1, 1), icpt_ref[0], jnp.float32)
 
     def weights(side, others, diagonal):
         product = lax.dot_general(
@@ -230,13 +257,24 @@
         got(REP, j)
         pass_inner(j).start()
 
-        @pl.when(inside)
+        @pl.when(stays(j))
         def _():
             pass_outer(j).start()
 
+    def turn_out(j):
+        got(OUT_NEAR, j)
+        shift_rep(j).start()
+
+    def turn_back(j):
+        got(OUT_FAR, j)
+        shift_back(j).start()
+
     def finish(j):
-        got(OUT_NEAR, j)
-        got(OUT_FAR, j)
+        @pl.when(jnp.logical_not(beside & (j >= PIECES - SHIFTED)))
+        def _():
+            got(OUT_NEAR, j)
+            got(OUT_FAR, j)
+
         got(IN_FAR, j)
         step(win[j, 0], win[j, 1])
 
@@ -254,6 +292,14 @@
         def _():
             serve(j)
 
+        @pl.when(beside & (j == SHIFT_OUT))
+        def _():
+            shifted(turn_out)
+
+        @pl.when(beside & (j == SHIFT_BACK))
+        def _():
+            shifted(turn_back)
+
         @pl.when(j < 2)
         def _():
             at = pl.ds(pl.multiple_of(j * half, half), half)
@@ -264,31 +310,40 @@
             finish(j - 1)
 
     each(PIECES + 1, body)
-    each(EXTRA, lambda j: step(win[j, 0], win[j, 1]))
+
+    def leave(a, out, part):
+        at = pl.ds(pl.multiple_of(part * CLOSE, CLOSE), CLOSE)
+        return pltpu.make_async_copy(res.at[a, at], out.at[at], out_sem.at[a, part])
 
     def close(a, out):
-        def part(j):
-            direction = raw[a, rows_of(j), :].astype(jnp.float32) * inv[a, rows_of(j), :]
-            upstream = acc[a, rows_of(j), :]
+        def part(k):
+            at = pl.ds(pl.multiple_of(k * CLOSE, CLOSE), CLOSE)
+            direction = raw[a, at, :].astype(jnp.float32) * inv[a, at, :]
+            upstream = acc[a, at, :]
             along = jnp.sum(upstream * direction, axis=1, keepdims=True)
-            res[a, rows_of(j), :] = (inv[a, rows_of(j), :] * (upstream - direction * along)).astype(jnp.bfloat16)
-            pltpu.make_async_copy(res.at[a, rows_of(j)], out.at[rows_of(j)], out_sem.at[a, j]).start()
-        each(PIECES, part)
+            out[at, :] = (inv[a, at, :] * (upstream - direction * along)).astype(jnp.bfloat16)
+        each(rows // CLOSE, part)
 
     close(1, gi_hbm)
     close(0, gc_hbm)
 
     def drain(j):
-        for a, out in ((1, gi_hbm), (0, gc_hbm)):
-            pltpu.make_async_copy(res.at[a, rows_of(j)], out.at[rows_of(j)], out_sem.at[a, j]).wait()
         to_inner(j).wait_send()
         pass_inner(j).wait_send()
 
         @pl.when(inside)
         def _():
+            to_outer(j).wait_send()
+
+        @pl.when(stays(j))
+        def _():
             to_rep(j).wait_send()
-            to_outer(j).wait_send()
             pass_outer(j).wait_send()
+
+        @pl.when(beside & (j >= PIECES - SHIFTED))
+        def _():
+            shift_rep(j).wait_send()
+            shift_back(j).wait_send()
 
         @pl.when(edge)
         def _():
@@ -314,12 +369,13 @@
         bf16, f32 = jnp.bfloat16, jnp.float32
         dma = pltpu.SemaphoreType.DMA
         vmem = pl.BlockSpec(memory_space=pltpu.VMEM)
+        smem = pl.BlockSpec(memory_space=pltpu.SMEM)
         anywhere = pl.BlockSpec(memory_space=pl.ANY)
         return pl.pallas_call(
             functools.partial(kernel, n_blk, 8),
-            out_shape=[jax.ShapeDtypeStruct((rows, width), bf16)] * 2,
-            in_specs=[vmem, vmem, anywhere, anywhere],
-            out_specs=[anywhere] * 2,
+            out_shape=[pltpu.VMEM((rows, width), bf16)] * 2,
+            in_specs=[smem, smem, anywhere, anywhere],
+            out_specs=[vmem] * 2,
             scratch_shapes=[
                 pltpu.VMEM((2, rows, width), bf16),
                 pltpu.VMEM((2, rows, 1), f32),
@@ -334,7 +390,7 @@
                 dma((4, PIECES)),
                 dma((PIECES,)),
                 dma((2, PIECES)),
-            ] + [dma((PIECES,))] * 7 + [dma((2, PIECES))],
+            ] + [dma((PIECES,))] * 7 + [dma((2, PIECES)), dma((PIECES,)), dma((PIECES,))],
             compiler_params=pltpu.CompilerParams(
                 collective_id=0, has_side_effects=True, vmem_limit_bytes=56 * 1024 * 1024
             ),
@@ -342,7 +398,7 @@
                 flops=24 * 2 * rows * rows * width, bytes_accessed=8 * rows * width, transcendentals=12 * rows * rows
             ),
         )(
-            exponent_of_scale.reshape(1, 1), additive_intercept.reshape(1, 1), photo_vectors, caption_vectors
+            exponent_of_scale, additive_intercept, photo_vectors, caption_vectors
         )
 
     whole = P(("blk", "rep"), None)

time: 91.6 us -> 86 us (0.939)
  the two profiles are of different devices: /device:TPU:8 before, /device:TPU:1 now
where the time goes in v3:
time: 86 us; the launch traced here: 85.9 us
  Pallas kernels  82 us (95%)
  local copies, waits for them, and re-layouts  2.03 us (2%)
  between operations  1.93 us (2%)
    pallas_call x1, Pallas kernels, shards(): pl.pallas_call(functools.partial(kernel, n_blk, 8), out_shape=[pltpu.VMEM...  82 us
    unnamed x2, local copies, waits for them, and re-layouts  2.03 us

profile of v3, /device:TPU:1, one launch (start us, length us, event | category | flops | bytes accessed | tf_op | source)
XLA Modules:
  0.0 85.9 jit_solution(10588301319621351046)
XLA Ops:
  1.9 82.0 %shard_map.59 = (bf16[512,1152]{1,0:T(8,128)(2,1)S(1)}, bf16[512,1152]{1,0:T(8,128)(2,1)S(1)}) custom-call(f32[1]{0:T(128)S(6)} %copy.10.exp_ref, f32[1]{0:T(128)S(6)} %copy.11.icpt_ref, bf16[512,1152]{1,0:T(8,128)(2,1)} %img_hbm.1, bf16[512,1152]{1,0:T(8,128)(2,1)} %cap_hbm.1), custom_call_target="tpu_custom_call" | custom-call | flops 14495514624 | bytes 4718592 | tf_op jit(solution)/shard_map/pallas_call | solution.py:374
  83.9 1.0 %copy.8 = bf16[512,1152]{1,0:T(8,128)(2,1)} copy(bf16[512,1152]{1,0:T(8,128)(2,1)S(1)} %get-tuple-element.2) | data formatting | bytes 2359296
  84.9 1.0 %copy.9 = bf16[512,1152]{1,0:T(8,128)(2,1)} copy(bf16[512,1152]{1,0:T(8,128)(2,1)S(1)} %get-tuple-element.3) | data formatting | bytes 2359296

commit v4 on v3

--- a/solution.py
+++ b/solution.py
@@ -9,7 +9,10 @@
 
 MESH = pl.DeviceIdType.MESH
 PIECES = 8
-SEND_AHEAD = 4
+EDGE_AHEAD = 4
+BEHIND_AHEAD = 1
+REP_AHEAD = 2
+OUT_AHEAD = 2
 RELAY_AHEAD = 2
 SHIFTED = 2
 SHIFT_OUT = 1
@@ -41,6 +44,8 @@
     beyond = lax.rem(pal + away + n_blk, n_blk)
     outer_low = lax.rem(outer // (2 * n_z), 2)
     source = outer + 2 * n_z * (1 - 2 * outer_low)
+    first_ahead = jnp.where(edge, EDGE_AHEAD, jnp.where(behind, BEHIND_AHEAD, REP_AHEAD))
+    second_ahead = jnp.where(edge, EDGE_AHEAD, OUT_AHEAD)
     rep_id = {"blk": blk, "rep": 1 - rep}
     inner_id = {"blk": inner, "rep": rep}
     outer_id = {"blk": outer, "rep": rep}
@@ -186,9 +191,12 @@
         for k in range(PREPARE):
             j = part * PREPARE + k
 
-            @pl.when(j < SEND_AHEAD)
+            @pl.when(j < first_ahead)
             def _():
                 send_first(j)
+
+            @pl.when(j < second_ahead)
+            def _():
                 send_second(j)
 
             to_inner(j).start()
@@ -245,10 +253,13 @@
             far_beyond(j).start()
 
     def serve(j):
-        @pl.when(j + SEND_AHEAD < PIECES)
-        def _():
-            send_first(j + SEND_AHEAD)
-            send_second(j + SEND_AHEAD)
+        @pl.when(j + first_ahead < PIECES)
+        def _():
+            send_first(j + first_ahead)
+
+        @pl.when(j + second_ahead < PIECES)
+        def _():
+            send_second(j + second_ahead)
 
         @pl.when(j + RELAY_AHEAD < PIECES)
         def _():

time: 86 us -> 81 us (0.942)
  Pallas kernels: 82 us -> 76.9 us
    pallas_call x1, Pallas kernels: 82 us -> 76.9 us  [shards(): pl.pallas_call(functools.partial(kernel, n_blk, 8), out_shape=[pltpu.VMEM...]
where the time goes in v4:
time: 81 us; the launch traced here: 80.8 us
  Pallas kernels  76.9 us (95%)
  local copies, waits for them, and re-layouts  2.03 us (3%)
  between operations  1.93 us (2%)
    pallas_call x1, Pallas kernels, shards(): pl.pallas_call(functools.partial(kernel, n_blk, 8), out_shape=[pltpu.VMEM...  76.9 us
    unnamed x2, local copies, waits for them, and re-layouts  2.03 us

profile of v4, /device:TPU:1, one launch (start us, length us, event | category | flops | bytes accessed | tf_op | source)
XLA Modules:
  0.0 80.8 jit_solution(458395069371798720)
XLA Ops:
  1.9 76.9 %shard_map.59 = (bf16[512,1152]{1,0:T(8,128)(2,1)S(1)}, bf16[512,1152]{1,0:T(8,128)(2,1)S(1)}) custom-call(f32[1]{0:T(128)S(6)} %copy.10.exp_ref, f32[1]{0:T(128)S(6)} %copy.11.icpt_ref, bf16[512,1152]{1,0:T(8,128)(2,1)} %img_hbm.1, bf16[512,1152]{1,0:T(8,128)(2,1)} %cap_hbm.1), custom_call_target="tpu_custom_call" | custom-call | flops 14495514624 | bytes 4718592 | tf_op jit(solution)/shard_map/pallas_call | solution.py:385
  78.8 1.0 %copy.8 = bf16[512,1152]{1,0:T(8,128)(2,1)} copy(bf16[512,1152]{1,0:T(8,128)(2,1)S(1)} %get-tuple-element.2) | data formatting | bytes 2359296
  79.8 1.0 %copy.9 = bf16[512,1152]{1,0:T(8,128)(2,1)} copy(bf16[512,1152]{1,0:T(8,128)(2,1)S(1)} %get-tuple-element.3) | data formatting | bytes 2359296

commit v5 on v4

--- a/solution.py
+++ b/solution.py
@@ -13,7 +13,9 @@
 BEHIND_AHEAD = 1
 REP_AHEAD = 2
 OUT_AHEAD = 2
+BESIDE_AHEAD = 3
 RELAY_AHEAD = 2
+SETTLED = 3
 SHIFTED = 2
 SHIFT_OUT = 1
 SHIFT_BACK = 3
@@ -45,7 +47,7 @@
     outer_low = lax.rem(outer // (2 * n_z), 2)
     source = outer + 2 * n_z * (1 - 2 * outer_low)
     first_ahead = jnp.where(edge, EDGE_AHEAD, jnp.where(behind, BEHIND_AHEAD, REP_AHEAD))
-    second_ahead = jnp.where(edge, EDGE_AHEAD, OUT_AHEAD)
+    second_ahead = jnp.where(edge, EDGE_AHEAD, jnp.where(beside, BESIDE_AHEAD, OUT_AHEAD))
     rep_id = {"blk": blk, "rep": 1 - rep}
     inner_id = {"blk": inner, "rep": rep}
     outer_id = {"blk": outer, "rep": rep}
@@ -239,18 +241,20 @@
             turn = lax.rem(j, 2) == rep
             got_relay(0, j)
 
+            near_beyond(j).start()
+
             @pl.when(turn)
             def _():
                 near_across(j).start()
 
-            near_beyond(j).start()
             got_relay(1, j)
+
+            far_beyond(j).start()
 
             @pl.when(turn)
             def _():
                 far_across(j).start()
 
-            far_beyond(j).start()
 
     def serve(j):
         @pl.when(j + first_ahead < PIECES)
@@ -290,14 +294,43 @@
         step(win[j, 0], win[j, 1])
 
     half = rows // 2
-    for k in range(RELAY_AHEAD):
-        hand_on(k)
-        if k < 2:
-            step(own[0, k * half:(k + 1) * half], own[1, k * half:(k + 1) * half], k * half, k == 0)
+    each(RELAY_AHEAD, hand_on)
+    for k in range(2):
+        step(own[0, k * half:(k + 1) * half], own[1, k * half:(k + 1) * half], k * half, k == 0)
 
     each(PIECES, lambda j: pltpu.make_async_copy(
         pdir.at[:, rows_of(j)], pdir.at[:, rows_of(j)], pdir_recv.at[j]).wait())
 
+    def drain(j):
+        to_inner(j).wait_send()
+        pass_inner(j).wait_send()
+
+        @pl.when(inside)
+        def _():
+            to_outer(j).wait_send()
+
+        @pl.when(stays(j))
+        def _():
+            to_rep(j).wait_send()
+            pass_outer(j).wait_send()
+
+        @pl.when(beside & (j >= PIECES - SHIFTED))
+        def _():
+            shift_rep(j).wait_send()
+            shift_back(j).wait_send()
+
+        @pl.when(edge)
+        def _():
+            to_near(j).wait_send()
+            to_far(j).wait_send()
+            near_beyond(j).wait_send()
+            far_beyond(j).wait_send()
+
+            @pl.when(lax.rem(j, 2) == rep)
+            def _():
+                near_across(j).wait_send()
+                far_across(j).wait_send()
+
     def body(j):
         @pl.when(j < PIECES)
         def _():
@@ -316,11 +349,16 @@
             at = pl.ds(pl.multiple_of(j * half, half), half)
             step(pdir[0, at, :], pdir[1, at, :])
 
+        @pl.when(j > SETTLED)
+        def _():
+            drain(j - 1 - SETTLED)
+
         @pl.when(j > 0)
         def _():
             finish(j - 1)
 
     each(PIECES + 1, body)
+    lax.fori_loop(PIECES - SETTLED, PIECES, lambda j, c: (drain(j), c)[1], 0)
 
     def leave(a, out, part):
         at = pl.ds(pl.multiple_of(part * CLOSE, CLOSE), CLOSE)
@@ -337,38 +375,6 @@
 
     close(1, gi_hbm)
     close(0, gc_hbm)
-
-    def drain(j):
-        to_inner(j).wait_send()
-        pass_inner(j).wait_send()
-
-        @pl.when(inside)
-        def _():
-            to_outer(j).wait_send()
-
-        @pl.when(stays(j))
-        def _():
-            to_rep(j).wait_send()
-            pass_outer(j).wait_send()
-
-        @pl.when(beside & (j >= PIECES - SHIFTED))
-        def _():
-            shift_rep(j).wait_send()
-            shift_back(j).wait_send()
-
-        @pl.when(edge)
-        def _():
-            to_near(j).wait_send()
-            to_far(j).wait_send()
-            near_beyond(j).wait_send()
-            far_beyond(j).wait_send()
-
-            @pl.when(lax.rem(j, 2) == rep)
-            def _():
-                near_across(j).wait_send()
-                far_across(j).wait_send()
-
-    each(PIECES, drain)
 
 
 def solution(mesh):

time: 81 us -> 80.8 us (level)
  no operation moved by 1% of the time
where the time goes in v5:
time: 80.8 us; the launch traced here: 80.7 us
  Pallas kernels  76.8 us (95%)
  local copies, waits for them, and re-layouts  2.03 us (3%)
  between operations  1.93 us (2%)
    pallas_call x1, Pallas kernels, shards(): pl.pallas_call(functools.partial(kernel, n_blk, 8), out_shape=[pltpu.VMEM...  76.8 us
    unnamed x2, local copies, waits for them, and re-layouts  2.03 us

profile of v5, /device:TPU:1, one launch (start us, length us, event | category | flops | bytes accessed | tf_op | source)
XLA Modules:
  0.0 80.7 jit_solution(6997872689446074453)
XLA Ops:
  1.9 76.8 %shard_map.59 = (bf16[512,1152]{1,0:T(8,128)(2,1)S(1)}, bf16[512,1152]{1,0:T(8,128)(2,1)S(1)}) custom-call(f32[1]{0:T(128)S(6)} %copy.10.exp_ref, f32[1]{0:T(128)S(6)} %copy.11.icpt_ref, bf16[512,1152]{1,0:T(8,128)(2,1)} %img_hbm.1, bf16[512,1152]{1,0:T(8,128)(2,1)} %cap_hbm.1), custom_call_target="tpu_custom_call" | custom-call | flops 14495514624 | bytes 4718592 | tf_op jit(solution)/shard_map/pallas_call | solution.py:391
  78.7 1.0 %copy.8 = bf16[512,1152]{1,0:T(8,128)(2,1)} copy(bf16[512,1152]{1,0:T(8,128)(2,1)S(1)} %get-tuple-element.2) | data formatting | bytes 2359296
  79.7 1.0 %copy.9 = bf16[512,1152]{1,0:T(8,128)(2,1)} copy(bf16[512,1152]{1,0:T(8,128)(2,1)S(1)} %get-tuple-element.3) | data formatting | bytes 2359296
